TPU v7x, 256 devices: a whole 4x4x8 slice. The times are simulated.
256 devices in a mesh: freq: 16 (over z, y_lo), orb: 16 (over x, y_hi, core).
Axes of the slice: x: 4, y: 4 (y_hi: 2, y_lo: 2; y = y_hi * 2 + y_lo), z: 8, core: 2. Of those that a mesh axis runs over, the one named last changes fastest.
Arguments:
- green: float32 [16, 2, 1024, 1024], P('freq', None, 'orb'), may hold values from -0.1875 to 0.1875
- green_bar: float32 [16, 2, 1024, 1024], P('freq', None, 'orb'), may hold values from -1.5 to 1.5
Outputs:
- h_bar: float32 [2, 1024, 1024], P(None, 'orb', 'freq')
All inputs are finite; a program needn't handle non-finite values.
Results may differ from a plain program's by a relative error of at most 0.0001.
Values sent between devices are 32-bit elements; how exact they have to be, the bound alone decides.
A program may use at most 64 MiB of HBM per device.

v0:
```python
import jax
import jax.numpy as jnp
from jax import lax
from jax.sharding import PartitionSpec as P


def complex_product(pattern, left_op, right_op):

    def real_dot(left_part, right_part):
        return jnp.einsum(
            pattern,
            left_part,
            right_part,
            precision=lax.Precision.HIGHEST,
            preferred_element_type=jnp.float32,
        )

    real_part = real_dot(left_op[0], right_op[0]) - real_dot(left_op[1], right_op[1])
    imag_part = real_dot(left_op[0], right_op[1]) + real_dot(left_op[1], right_op[0])
    return jnp.stack([real_part, imag_part])


def body(green, green_bar):
    row_count = green.shape[2]
    green_now = green[0]
    bar_now = green_bar[0]
    gathered = lax.all_gather(green_now, "orb", axis=1, tiled=True)
    middle = complex_product("ik,jk->ij", bar_now, gathered)
    own_columns = lax.dynamic_slice_in_dim(
        gathered, lax.axis_index("orb") * row_count, row_count, 2
    )
    adjoint = complex_product(
        "ki,kj->ij", own_columns, lax.all_gather(middle, "orb", axis=1, tiled=True)
    )
    return lax.psum_scatter(adjoint, "freq", scatter_dimension=2, tiled=True)


def solution(mesh):
    in_specs = (P("freq", None, "orb", None), P("freq", None, "orb", None))
    out_specs = P(None, "orb", "freq")
    return jax.shard_map(body, mesh=mesh, in_specs=in_specs, out_specs=out_specs, check_vma=False)
```

profile of v0, /device:TPU:6, one launch (start us, length us, event | category | flops | bytes accessed | tf_op | source)
XLA Modules:
  0.0 285.6 jit_solution(7644064740732199588)
XLA Ops:
  6.5 0.0 copy-start.2
  6.5 0.0 all-gather.6.cloned.1.call-start
  6.5 0.7 all-gather.6.cloned.1.call-update
  7.3 0.0 all-gather.4.cloned.1.call-start
  7.3 81.7 %all-gather.6.cloned.1.call-done = f32[1,2,1024,1024]{3,2,1,0:T(8,128)} async-done(((f32[1,2,64,1024]{3,2,1,0:T(8,128)}), f32[1,2,1024,1024]{3,2,1,0:T(8,128)}) %all-gather.6.cloned.1.call-update) | async-done | bytes 8388624 | tf_op jit(solution)/shard_map/all_gather | solution.py:27
  89.0 0.0 copy-start
  89.0 6.5 %fusion.1 = f32[64,1024]{1,0:T(8,128)S(1)} fusion(f32[1,2,1024,1024]{3,2,1,0:T(8,128)} %all-gather.6.cloned.1.call-done, f32[1,2,64,1024]{3,2,1,0:T(8,128)} %param.3), kind=kOutput, calls=%fused_computation.5 | convolution fusion | flops 805306368 | bytes 4718592 | tf_op jit(solution)/shard_map/ik,jk->ij/dot_general | solution.py:10
  95.5 6.4 %fusion = f32[64,1024]{1,0:T(8,128)S(1)} fusion(f32[1,2,1024,1024]{3,2,1,0:T(8,128)} %all-gather.6.cloned.1.call-done, f32[1,2,64,1024]{3,2,1,0:T(8,128)} %param.3), kind=kOutput, calls=%fused_computation.4 | convolution fusion | flops 805306368 | bytes 4718592 | tf_op jit(solution)/shard_map/ik,jk->ij/dot_general | solution.py:10
  101.9 0.0 copy-done.2
  101.9 0.0 copy-done
  101.9 4.2 %fusion.13 = f32[1,64,1024]{2,1,0:T(8,128)S(1)} fusion(f32[64,1024]{1,0:T(8,128)S(1)} %fusion.1, f32[1,2,1024,1024]{3,2,1,0:T(8,128)S(1)} %copy-done, f32[1,2,64,1024]{3,2,1,0:T(8,128)S(1)} %copy-done.2), kind=kOutput, calls=%fused_computation.17 | convolution fusion | flops 805371904 | bytes 4980736 | tf_op jit(solution)/shard_map/ik,jk->ij/dot_general | solution.py:10
  106.1 4.3 %fusion.15 = f32[1,64,1024]{2,1,0:T(8,128)S(1)} fusion(f32[64,1024]{1,0:T(8,128)S(1)} %fusion, f32[1,2,1024,1024]{3,2,1,0:T(8,128)S(1)} %copy-done, f32[1,2,64,1024]{3,2,1,0:T(8,128)S(1)} %copy-done.2), kind=kOutput, calls=%fused_computation.19 | convolution fusion | flops 805371904 | bytes 4980736 | tf_op jit(solution)/shard_map/ik,jk->ij/dot_general | solution.py:10
  110.4 0.8 pad_maximum_fusion
  111.2 0.0 all-gather.4.cloned.1.call-update
  111.2 0.0 reduce-scatter.4.cloned.1.call-start
  111.3 75.8 %all-gather.4.cloned.1.call-done = f32[2,1024,1024]{2,1,0:T(8,128)} async-done(((f32[2,64,1024]{2,1,0:T(8,128)}), f32[2,1024,1024]{2,1,0:T(8,128)}) %all-gather.4.cloned.1.call-update) | async-done | bytes 8388624 | tf_op jit(solution)/shard_map/all_gather | solution.py:33
  187.1 0.0 copy-start.1
  187.1 5.3 %fusion.5 = f32[64,1024]{1,0:T(8,128)S(1)} fusion(f32[2,1024,1024]{2,1,0:T(8,128)} %all-gather.4.cloned.1.call-done, f32[1,2,1024,1024]{3,2,1,0:T(8,128)} %all-gather.6.cloned.1.call-done, s32[]{:T(128)S(6)} %select_n.3), kind=kOutput, calls=%fused_computation.9 | convolution fusion | flops 805306368 | bytes 4980740 | tf_op jit(solution)/shard_map/ki,kj->ij/dot_general | solution.py:10
  192.4 5.1 %fusion.4 = f32[64,1024]{1,0:T(8,128)S(1)} fusion(f32[2,1024,1024]{2,1,0:T(8,128)} %all-gather.4.cloned.1.call-done, f32[1,2,1024,1024]{3,2,1,0:T(8,128)} %all-gather.6.cloned.1.call-done, s32[]{:T(128)S(6)} %add.14, s32[]{:T(128)S(6)} %select_n.3), kind=kOutput, calls=%fused_computation.8 | convolution fusion | flops 805306368 | bytes 4980744 | tf_op jit(solution)/shard_map/ki,kj->ij/dot_general | solution.py:10
  197.5 0.0 copy-done.1
  197.5 3.8 %fusion.9 = f32[1,64,1024]{2,1,0:T(8,128)S(1)} fusion(f32[64,1024]{1,0:T(8,128)S(1)} %fusion.5, f32[2,1024,1024]{2,1,0:T(8,128)S(1)} %copy-done.1, f32[1,2,1024,1024]{3,2,1,0:T(8,128)} %all-gather.6.cloned.1.call-done, s32[]{:T(128)S(6)} %add.14, s32[]{:T(128)S(6)} %select_n.3), kind=kOutput, calls=%fused_computation.13 | convolution fusion | flops 805371904 | bytes 5242888 | tf_op jit(solution)/shard_map/ki,kj->ij/dot_general | solution.py:10
  201.4 3.8 %fusion.11 = f32[1,64,1024]{2,1,0:T(8,128)S(1)} fusion(f32[64,1024]{1,0:T(8,128)S(1)} %fusion.4, f32[2,1024,1024]{2,1,0:T(8,128)S(1)} %copy-done.1, f32[1,2,1024,1024]{3,2,1,0:T(8,128)} %all-gather.6.cloned.1.call-done, s32[]{:T(128)S(6)} %select_n.3), kind=kOutput, calls=%fused_computation.15 | convolution fusion | flops 805371904 | bytes 5242884 | tf_op jit(solution)/shard_map/ki,kj->ij/dot_general | solution.py:10
  205.2 0.6 copy.3
  205.8 1.4 reshape.14
  207.2 0.0 reduce-scatter.4.cloned.1.call-update
  207.2 70.2 %reduce-scatter.4.cloned.1.call-done = f32[64,128]{1,0:T(8,128)} async-done(((f32[1024,128]{1,0:T(8,128)}), f32[64,128]{1,0:T(8,128)}) %reduce-scatter.4.cloned.1.call-update) | async-done | bytes 32784
  277.5 0.9 reshape.15
  278.3 0.7 copy.4
  (1 shorter events, 0.0 us)
Async XLA Ops:
  6.5 95.3 %copy-start.2 = (f32[1,2,64,1024]{3,2,1,0:T(8,128)S(1)}, f32[1,2,64,1024]{3,2,1,0:T(8,128)}, u32[]{:S(2)}) copy-start(f32[1,2,64,1024]{3,2,1,0:T(8,128)} %param.3) | copy-start | bytes 1572868
  6.5 82.5 %all-gather.6.cloned.1.call-start = ((), (), s32[]{:S(2)}) async-start(), calls=%async_computation.2 | async-start | bytes 8912896 | tf_op jit(solution)/shard_map/all_gather | solution.py:27
  7.3 179.9 %all-gather.4.cloned.1.call-start = ((), (), s32[]{:S(2)}) async-start(), calls=%async_computation.1 | async-start | bytes 8912896 | tf_op jit(solution)/shard_map/all_gather | solution.py:33
  89.0 12.8 %copy-start = (f32[1,2,1024,1024]{3,2,1,0:T(8,128)S(1)}, f32[1,2,1024,1024]{3,2,1,0:T(8,128)}, u32[]{:S(2)}) copy-start(f32[1,2,1024,1024]{3,2,1,0:T(8,128)} %all-gather.6.cloned.1.call-done) | copy-start | bytes 25165828
  111.2 166.2 %reduce-scatter.4.cloned.1.call-start = ((), (), s32[]{:S(2)}) async-start(), calls=%async_computation.3 | async-start | bytes 557056
  187.1 10.4 %copy-start.1 = (f32[2,1024,1024]{2,1,0:T(8,128)S(1)}, f32[2,1024,1024]{2,1,0:T(8,128)}, u32[]{:S(2)}) copy-start(f32[2,1024,1024]{2,1,0:T(8,128)} %all-gather.4.cloned.1.call-done) | copy-start | bytes 25165828
Sparse Core Ops, SparseCore 0:
  10.1 78.8 all-gather.5
  111.4 75.7 all-gather.3
  207.4 70.0 reduce-scatter.3
where the time goes:
time: 286 us
  waiting for transfers between devices  229 us (80%)
  matrix products  39.4 us (14%)
  between operations  13.2 us (5%)
  local copies, waits for them, and re-layouts  3.54 us (1%)
    all_gather x1, waiting for transfers between devices, body(): gathered = lax.all_gather(green_now, 'orb', axis=1, tiled=True)  81.7 us
    all_gather x1, waiting for transfers between devices, body(): lax.all_gather(middle, 'orb', axis=1, tiled=True)  75.8 us
    unnamed x4, waiting for transfers between devices  71 us
    dot_general x8, matrix products, real_dot(): jnp.einsum(pattern, left_part, right_part, precision=lax.Precision.HIGHES...  39.4 us
  transfers between devices with their start and end apart: 3, of which 3 were waited for; matrix products, arithmetic and copies ran while one was open for 0% of the time, Pallas kernels for 0%

commit v1 on v0

v1 whole, which is shorter than its diff:
```python
import jax
import jax.numpy as jnp
from jax import lax
from jax.experimental import pallas as pl
from jax.experimental.pallas import tpu as pltpu
from jax.sharding import PartitionSpec as P

ROWS = 64
N = 1024
GROUPS = 4
UNIT = 128
X, Z = 4, 8

XP, XM, XF, CB, CG, YB, CBF, YG, CGF, ZC, FIN = 0, 2, 4, 6, 7, 8, 10, 12, 16, 20, 48
COPIES = 56


def split(value):
    high = value.astype(jnp.bfloat16)
    return high, (value - high.astype(jnp.float32)).astype(jnp.bfloat16)


def matmul(left, right, transposed):
    dims = (((1,), (1 if transposed else 0,)), ((), ()))
    return lax.dot_general(left, right, dims, preferred_element_type=jnp.float32)


def three_pass(left_hi, left_lo, right_hi, right_lo, transposed):
    return (
        matmul(left_hi, right_hi, transposed)
        + matmul(left_hi, right_lo, transposed)
        + matmul(left_lo, right_hi, transposed)
    )


def device_at(x, h, z, low, core):
    return {"freq": z * 2 + low, "orb": x * 4 + h * 2 + core}


def kernel(
    g_ref, b_ref, out_ref,
    gc, ba, ga, l_hi, l_lo, w_hi, w_lo, a_hi, a_lo, part, zr, fs, fr,
    send, recv, fin,
):
    freq, orb = lax.axis_index("freq"), lax.axis_index("orb")
    z, low = freq // 2, freq % 2
    x, h, core = orb // 4, (orb // 2) % 2, orb % 2
    odd = z % 2

    x_next = device_at((x + 1) % X, h, z, low, core)
    x_prev = device_at((x + 3) % X, h, z, low, core)
    partner = device_at(x, 1 - h, z, low, core)
    other = device_at(x, h, z, low, 1 - core)
    z_next = device_at(x, h, (z + 1) % Z, low, core)
    z_prev = device_at(x, h, (z + 7) % Z, low, core)

    def owner(group, half):
        return device_at(group, odd, 2 * (z // 2) + h, core, half)

    def owner_is_me(group, half):
        return (x == group) & (h == odd) & (low == core) & (core == half)

    def copy(src, dst, number, target):
        return pltpu.make_async_remote_copy(
            src_ref=src, dst_ref=dst, send_sem=send.at[number], recv_sem=recv.at[number],
            device_id=target, device_id_type=pl.DeviceIdType.MESH,
        )

    barrier = pltpu.get_barrier_semaphore()

    def greet(target):
        pl.semaphore_signal(barrier, inc=1, device_id=target, device_id_type=pl.DeviceIdType.MESH)

    for target in (x_next, x_prev, partner, other, z_next, z_prev):
        greet(target)
    self_owner = (h == odd) & (low == core)
    for from_x in range(X):
        for from_low in range(2):
            itself = self_owner & (x == from_x) & (low == from_low)

            @pl.when(jnp.logical_not(itself))
            def _():
                greet(device_at(from_x, odd, 2 * (z // 2) + h, from_low, low))

    pl.semaphore_wait(barrier, 14 - self_owner.astype(jnp.int32))

    g, b = g_ref.at[0], b_ref.at[0]
    xp = [copy(g.at[p], gc.at[0, p], XP + p, x_next) for p in range(2)]
    xm = [copy(g.at[p], gc.at[1, p], XM + p, x_prev) for p in range(2)]
    xf = [copy(gc.at[0, 0], gc.at[2, 0], XF, x_next), copy(gc.at[1, 1], gc.at[2, 1], XF + 1, x_prev)]
    yb = [copy(b.at[p], ba.at[1, p], YB + p, partner) for p in range(2)]
    cb = copy(b, ba.at[0], CB, other)
    cg = copy(g, ga.at[0], CG, other)
    cbf = [copy(ba.at[1, p], ba.at[2, p], CBF + p, other) for p in range(2)]

    def lanes(group):
        return pl.ds(group * 256, 256)

    yg = [copy(g.at[:, :, lanes(i)], ga.at[1, :, :, lanes(i)], YG + i, partner) for i in range(GROUPS)]
    cgf = [copy(ga.at[1, :, :, lanes(i)], ga.at[2, :, :, lanes(i)], CGF + i, other) for i in range(GROUPS)]

    yb[0].start()
    xp[0].start()
    xm[1].start()
    cb.start()
    yb[1].start()
    xp[1].start()
    xm[0].start()
    cg.start()

    def fill_left(ref, from_x):
        high_r, low_r = split(ref[0])
        high_i, low_i = split(ref[1])
        top = pl.ds(pl.multiple_of(from_x * ROWS, ROWS), ROWS)
        bottom = pl.ds(pl.multiple_of(256 + from_x * ROWS, ROWS), ROWS)
        for dst, re, im in ((l_hi, high_r, high_i), (l_lo, low_r, low_i)):
            dst[top, :N] = re
            dst[top, N:] = -im
            dst[bottom, :N] = im
            dst[bottom, N:] = re

    def fill_bar(ref, slot):
        rows = pl.ds(slot * ROWS, ROWS)
        for p in range(2):
            w_hi[rows, pl.ds(p * N, N)], w_lo[rows, pl.ds(p * N, N)] = split(ref[p])

    def fill_rows(ref, slot, columns):
        for p in range(2):
            rows = pl.ds(p * 256 + slot * ROWS, ROWS)
            a_hi[rows, columns], a_lo[rows, columns] = split(ref[p, :, columns])

    fill_left(g, x)
    fill_bar(b, 0)
    fill_rows(g, 0, pl.ds(0, N))
    cb.wait_recv()
    fill_bar(ba.at[0], 1)
    cg.wait_recv()
    fill_rows(ga.at[0], 1, pl.ds(0, N))

    yb[0].wait_send()
    yg[0].start()
    xp[0].wait_recv()
    xf[0].start()
    xm[1].wait_recv()
    xf[1].start()
    yb[0].wait_recv()
    cbf[0].start()
    yb[1].wait_send()
    yg[1].start()
    yb[1].wait_recv()
    cbf[1].start()
    fill_bar(ba.at[1], 2)
    xp[1].wait_recv()
    fill_left(gc.at[0], (x + 3) % X)
    xm[0].wait_recv()
    fill_left(gc.at[1], (x + 1) % X)
    for c in cbf:
        c.wait_recv()
    fill_bar(ba.at[2], 3)
    yg[0].wait_recv()
    cgf[0].start()
    yg[0].wait_send()
    yg[2].start()
    for c in xf:
        c.wait_recv()
    fill_left(gc.at[2], (x + 2) % X)

    middle = three_pass(l_hi[...], l_lo[...], w_hi[...], w_lo[...], True)
    m_r, m_i = middle[:256], middle[256:]
    left = jnp.concatenate(
        [jnp.concatenate([m_r, -m_i], axis=1), jnp.concatenate([m_i, m_r], axis=1)], axis=0
    )
    left_hi, left_lo = split(left)
    l_hi[:, :512] = left_hi
    l_lo[:, :512] = left_lo

    def chain(group):
        sign = 1 if group % 2 == 0 else -1
        chains = []
        first = ZC + group * 7
        for direction, hops, base in ((sign, 4, 0), (-sign, 3, 4)):
            target = z_next if direction == 1 else z_prev
            steps = []
            for s in range(hops):
                dest = (z + direction * (hops - s) + Z) % Z
                src = part.at[group, dest] if s == 0 else zr.at[group, base + s - 1]
                steps.append((copy(src, zr.at[group, base + s], first + base + s, target), dest, base + s - 1))
            chains.append(steps)
        return chains

    chains = [chain(i) for i in range(GROUPS)]

    def advance(group, s):
        for steps in chains[group]:
            if s < len(steps):
                step, dest, before = steps[s]
                if s > 0:
                    steps[s - 1][0].wait_recv()
                    zr[group, before] += part[group, dest]
                step.start()

    def owner_copy(group, half):
        place = x * 2 + low
        src, dst = fs.at[group, pl.ds(half * ROWS, ROWS)], fr.at[place]
        remote = pltpu.make_async_remote_copy(
            src_ref=src, dst_ref=dst, send_sem=send.at[FIN + group * 2 + half], recv_sem=fin.at[place],
            device_id=owner(group, half), device_id_type=pl.DeviceIdType.MESH,
        )
        return remote, pltpu.make_async_copy(src, dst, fin.at[place])

    def finish(group):
        for steps in chains[group]:
            steps[-1][0].wait_recv()
        total = part[group, z] + zr[group, 3] + zr[group, 6]
        fs[group] = total.T
        for half in range(2):
            remote, local = owner_copy(group, half)
            itself = owner_is_me(group, half)

            @pl.when(itself)
            def _():
                local.start()

            @pl.when(jnp.logical_not(itself))
            def _():
                remote.start()

    for tick in range(GROUPS + 4):
        if tick < GROUPS:
            cols = lanes(tick)
            if tick > 0:
                yg[tick].wait_recv()
                cgf[tick].start()
            if tick == 0:
                yg[1].wait_send()
                yg[3].start()
            fill_rows(ga.at[1], 2, cols)
            cgf[tick].wait_recv()
            fill_rows(ga.at[2], 3, cols)
            total = three_pass(l_hi[:, :512], l_lo[:, :512], a_hi[:, cols], a_lo[:, cols], False)
            for to_x in range(X):
                for to_h in range(2):
                    columns = slice(to_h * UNIT, (to_h + 1) * UNIT)
                    part[tick, 2 * to_x + to_h, :ROWS] = total[to_x * ROWS:(to_x + 1) * ROWS, columns]
                    part[tick, 2 * to_x + to_h, ROWS:] = total[256 + to_x * ROWS:256 + (to_x + 1) * ROWS, columns]
            advance(tick, 0)
        for group in range(GROUPS):
            s = tick - group
            if 1 <= s <= 3:
                advance(group, s)
            elif s == 4:
                finish(group)

    for place in range(8):
        pltpu.make_async_remote_copy(
            src_ref=fs.at[0, pl.ds(0, ROWS)], dst_ref=fr.at[place], send_sem=send.at[FIN], recv_sem=fin.at[place],
            device_id=other, device_id_type=pl.DeviceIdType.MESH,
        ).wait_recv()
    total = fr[0]
    for place in range(1, 8):
        total = total + fr[place]
    out_ref[0] = total[:, :ROWS]
    out_ref[1] = total[:, ROWS:]

    for c in (*xp, *xm, *xf, cb, cg, yg[2], yg[3], *cbf, *cgf):
        c.wait_send()
    for group in range(GROUPS):
        for steps in chains[group]:
            for step, _, _ in steps:
                step.wait_send()
        for half in range(2):
            @pl.when(jnp.logical_not(owner_is_me(group, half)))
            def _():
                owner_copy(group, half)[0].wait_send()


def body(green, green_bar):
    f32, bf16 = jnp.float32, jnp.bfloat16
    vmem = pl.BlockSpec(memory_space=pltpu.VMEM)
    return pl.pallas_call(
        kernel,
        out_shape=jax.ShapeDtypeStruct((2, ROWS, ROWS), f32),
        in_specs=[vmem, vmem],
        out_specs=vmem,
        scratch_shapes=[
            pltpu.VMEM((3, 2, ROWS, N), f32),
            pltpu.VMEM((3, 2, ROWS, N), f32),
            pltpu.VMEM((3, 2, ROWS, N), f32),
            pltpu.VMEM((512, 2 * N), bf16),
            pltpu.VMEM((512, 2 * N), bf16),
            pltpu.VMEM((256, 2 * N), bf16),
            pltpu.VMEM((256, 2 * N), bf16),
            pltpu.VMEM((512, N), bf16),
            pltpu.VMEM((512, N), bf16),
            pltpu.VMEM((GROUPS, Z, UNIT, UNIT), f32),
            pltpu.VMEM((GROUPS, 7, UNIT, UNIT), f32),
            pltpu.VMEM((GROUPS, UNIT, UNIT), f32),
            pltpu.VMEM((8, ROWS, UNIT), f32),
            pltpu.SemaphoreType.DMA((COPIES,)),
            pltpu.SemaphoreType.DMA((COPIES,)),
            pltpu.SemaphoreType.DMA((8,)),
        ],
        compiler_params=pltpu.CompilerParams(
            collective_id=0, has_side_effects=True, vmem_limit_bytes=40 * 1024 * 1024
        ),
        cost_estimate=pl.CostEstimate(flops=3 * 1073741824, bytes_accessed=1081344, transcendentals=0),
        name="dyson_adjoint",
    )(green, green_bar)


def solution(mesh):
    spec = P("freq", None, "orb", None)
    return jax.shard_map(
        body, mesh=mesh, in_specs=(spec, spec), out_specs=P(None, "orb", "freq"), check_vma=False
    )
```

time: 286 us -> 73.1 us (0.26)
  the two profiles are of different devices: /device:TPU:6 before, /device:TPU:39 now
where the time goes in v1:
time: 73.1 us; the launch traced here: 73 us
  Pallas kernels  70.2 us (96%)
  local copies, waits for them, and re-layouts  2.71 us (4%)
    pallas_call x1, Pallas kernels, body(): pl.pallas_call(kernel, out_shape=jax.ShapeDtypeStruct((2, ROWS, ROWS), f3...  70.2 us
    unnamed x5, local copies, waits for them, and re-layouts  2.71 us

profile of v1, /device:TPU:39, one launch (start us, length us, event | category | flops | bytes accessed | tf_op | source)
XLA Modules:
  0.0 73.0 jit_solution(13613098359328618435)
XLA Ops:
  0.0 0.0 copy-start
  0.0 1.0 %copy-done = f32[1,2,64,1024]{3,2,1,0:T(8,128)S(1)} copy-done((f32[1,2,64,1024]{3,2,1,0:T(8,128)S(1)}, f32[1,2,64,1024]{3,2,1,0:T(8,128)}, u32[]{:S(2)}) %copy-start) | copy-done | bytes 524312
  1.0 0.0 copy-start.1
  1.0 1.0 %copy-done.1 = f32[1,2,64,1024]{3,2,1,0:T(8,128)S(1)} copy-done((f32[1,2,64,1024]{3,2,1,0:T(8,128)S(1)}, f32[1,2,64,1024]{3,2,1,0:T(8,128)}, u32[]{:S(2)}) %copy-start.1) | copy-done | bytes 524312
  2.1 70.2 %dyson_adjoint.1 = f32[2,64,64]{2,1,0:T(8,128)S(1)} custom-call(f32[1,2,64,1024]{3,2,1,0:T(8,128)S(1)} %copy-done, f32[1,2,64,1024]{3,2,1,0:T(8,128)S(1)} %copy-done.1), custom_call_target="tpu_custom_call" | custom-call | flops 3221225472 | bytes 1081344 | tf_op jit(solution)/shard_map/dyson_adjoint/pallas_call | solution.py:280
  72.3 0.6 copy.4
Async XLA Ops:
  0.0 1.0 %copy-start = (f32[1,2,64,1024]{3,2,1,0:T(8,128)S(1)}, f32[1,2,64,1024]{3,2,1,0:T(8,128)}, u32[]{:S(2)}) copy-start(f32[1,2,64,1024]{3,2,1,0:T(8,128)} %g_ref.1) | copy-start | bytes 1572868
  1.0 1.0 %copy-start.1 = (f32[1,2,64,1024]{3,2,1,0:T(8,128)S(1)}, f32[1,2,64,1024]{3,2,1,0:T(8,128)}, u32[]{:S(2)}) copy-start(f32[1,2,64,1024]{3,2,1,0:T(8,128)} %b_ref.1) | copy-start | bytes 1572868

commit v2 on v1

v2 whole, which is shorter than its diff:
```python
import jax
import jax.numpy as jnp
from jax import lax
from jax.experimental import pallas as pl
from jax.experimental.pallas import tpu as pltpu
from jax.sharding import PartitionSpec as P

ROWS = 64
N = 1024
GROUPS = 4
WIDE = 256
LANES = 128
X, Z = 4, 8
HOPS = 7
COPIES = 120


def split(value):
    high = value.astype(jnp.bfloat16)
    return high, (value - high.astype(jnp.float32)).astype(jnp.bfloat16)


def matmul(left, right, transposed):
    dims = (((1,), (1 if transposed else 0,)), ((), ()))
    return lax.dot_general(left, right, dims, preferred_element_type=jnp.float32)


def three_pass(left_hi, left_lo, right_hi, right_lo, transposed):
    return (
        matmul(left_hi, right_hi, transposed)
        + matmul(left_hi, right_lo, transposed)
        + matmul(left_lo, right_hi, transposed)
    )


def device_at(x, h, z, low, core):
    return {"freq": z * 2 + low, "orb": x * 4 + h * 2 + core}


def kernel(
    g_hbm, b_hbm, out_ref,
    g, b, gc, ba, ga, l_hi, l_lo, w_hi, w_lo, m_hi, m_lo, a_hi, a_lo,
    part_z, part_x, got_z, got_x, sum_x, hop_x, own_z, own_x, end_z, end_x, turn,
    send, recv, fin_z, fin_x, load,
):
    freq, orb = lax.axis_index("freq"), lax.axis_index("orb")
    z, low = freq // 2, freq % 2
    x, h, core = orb // 4, (orb // 2) % 2, orb % 2
    odd, pair = z % 2, z // 2

    x_next = device_at((x + 1) % X, h, z, low, core)
    x_far = device_at((x + 2) % X, h, z, low, core)
    x_prev = device_at((x + 3) % X, h, z, low, core)
    partner = device_at(x, 1 - h, z, low, core)
    other = device_at(x, h, z, low, 1 - core)
    z_next = device_at(x, h, (z + 1) % Z, low, core)
    z_prev = device_at(x, h, (z + 7) % Z, low, core)

    load_g = pltpu.make_async_copy(g_hbm.at[0], g, load.at[0])
    load_b = pltpu.make_async_copy(b_hbm.at[0], b, load.at[1])
    load_g.start()
    load_b.start()

    numbers = iter(range(COPIES))

    def copy(src, dst, target):
        number = next(numbers)
        return pltpu.make_async_remote_copy(
            src_ref=src, dst_ref=dst, send_sem=send.at[number], recv_sem=recv.at[number],
            device_id=target, device_id_type=pl.DeviceIdType.MESH,
        )

    barrier = pltpu.get_barrier_semaphore()

    def greet(target):
        pl.semaphore_signal(barrier, inc=1, device_id=target, device_id_type=pl.DeviceIdType.MESH)

    def greet_unless(itself, target):
        @pl.when(jnp.logical_not(itself))
        def _():
            greet(target)

    for target in (x_next, x_prev, x_far, partner, other, z_next, z_prev):
        greet(target)
    self_z = (h == odd) & (low == core)
    self_x = self_z & (x == pair)
    for from_x in range(X):
        for from_low in range(2):
            greet_unless(
                self_z & (x == from_x) & (low == from_low),
                device_at(from_x, odd, 2 * pair + h, from_low, low),
            )
    for from_pair in range(Z // 2):
        for from_low in range(2):
            greet_unless(
                self_x & (pair == from_pair) & (low == from_low),
                device_at(pair, odd, 2 * from_pair + h, from_low, low),
            )
    pl.semaphore_wait(barrier, 23 - self_z.astype(jnp.int32) - self_x.astype(jnp.int32))

    def wide(group):
        return pl.ds(group * WIDE, WIDE)

    gh, bh = g_hbm.at[0], b_hbm.at[0]
    yb = [copy(bh.at[p], ba.at[1, p], partner) for p in range(2)]
    xp = [copy(gh.at[p], gc.at[0, p], x_next) for p in range(2)]
    xm = [copy(gh.at[p], gc.at[1, p], x_prev) for p in range(2)]
    cb = copy(bh, ba.at[0], other)
    cg = copy(gh, ga.at[0], other)
    yg = [copy(gh.at[:, :, wide(i)], ga.at[1, :, :, wide(i)], partner) for i in range(GROUPS)]
    for c in (yb[0], xp[0], xm[1], cb, yb[1], xp[1], xm[0], cg, *yg):
        c.start()
    xf = [copy(gc.at[0, 0], gc.at[2, 0], x_next), copy(gc.at[1, 1], gc.at[2, 1], x_prev)]
    cbf = [copy(ba.at[1, p], ba.at[2, p], other) for p in range(2)]
    cgf = [copy(ga.at[1, :, :, wide(i)], ga.at[2, :, :, wide(i)], other) for i in range(GROUPS)]

    def fill_left(ref, place):
        high_r, low_r = split(ref[0])
        high_i, low_i = split(ref[1])
        for dst, re, im in ((l_hi, high_r, high_i), (l_lo, low_r, low_i)):
            for half in range(2):
                rows = slice(half * 32, half * 32 + 32)
                top = pl.ds(place * 128 + half * 64, 32)
                bottom = pl.ds(place * 128 + half * 64 + 32, 32)
                dst[top, :N] = re[rows]
                dst[top, N:] = -im[rows]
                dst[bottom, :N] = im[rows]
                dst[bottom, N:] = re[rows]

    def fill_bar(ref, slot):
        rows = pl.ds(slot * ROWS, ROWS)
        for p in range(2):
            w_hi[rows, pl.ds(p * N, N)], w_lo[rows, pl.ds(p * N, N)] = split(ref[p])

    def fill_rows(ref, slot, columns):
        for p in range(2):
            rows = pl.ds(p * 256 + slot * ROWS, ROWS)
            a_hi[rows, columns], a_lo[rows, columns] = split(ref[p, :, columns])

    def middle(start, count):
        rows = pl.ds(start * 128, count * 128)
        product = three_pass(l_hi[rows, :], l_lo[rows, :], w_hi[...], w_lo[...], True)
        for piece in range(start * 2, (start + count) * 2):
            at = (piece - start * 2) * 64
            re, im = product[at:at + 32], product[at + 32:at + 64]
            for first, second, rows in ((re, -im, pl.ds(piece * 64, 32)), (im, re, pl.ds(piece * 64 + 32, 32))):
                m_hi[rows, :256], m_lo[rows, :256] = split(first)
                m_hi[rows, 256:], m_lo[rows, 256:] = split(second)

    load_g.wait()
    fill_left(g, 0)
    fill_rows(g, 0, pl.ds(0, N))
    load_b.wait()
    fill_bar(b, 0)
    cb.wait_recv()
    fill_bar(ba.at[0], 1)
    cg.wait_recv()
    fill_rows(ga.at[0], 1, pl.ds(0, N))

    xp[0].wait_recv()
    xf[0].start()
    xm[1].wait_recv()
    xf[1].start()
    yb[0].wait_recv()
    cbf[0].start()
    xp[1].wait_recv()
    fill_left(gc.at[0], 2)
    xm[0].wait_recv()
    fill_left(gc.at[1], 1)
    yb[1].wait_recv()
    cbf[1].start()
    fill_bar(ba.at[1], 2)
    for c in cbf:
        c.wait_recv()
    fill_bar(ba.at[2], 3)
    middle(0, 3)
    yg[0].wait_recv()
    cgf[0].start()
    for c in xf:
        c.wait_recv()
    fill_left(gc.at[2], 3)
    middle(3, 1)

    def chains_of(group, own_part, got):
        sign = 1 if group % 2 == 0 else -1
        chains = []
        for direction, hops, base in ((sign, 4, 0), (-sign, 3, 4)):
            target = z_next if direction == 1 else z_prev
            steps = []
            for s in range(hops):
                dest = (z + direction * (hops - s) + Z) % Z
                before = got.at[group, base + s - 1]
                steps.append((copy(own_part(dest) if s == 0 else before, got.at[group, base + s], target), dest, before))
            chains.append(steps)
        return chains

    def unit_z(group):
        return lambda dest: part_z.at[group, ((dest // 2 - x + X) % X) * 2 + dest % 2]

    def unit_x(group):
        return lambda dest: hop_x.at[group, dest]

    chains_z = [chains_of(i, unit_z(i), got_z) for i in range(GROUPS)]
    chains_x = [chains_of(i, unit_x(i), got_x) for i in range(GROUPS)]
    to_x = [
        [copy(part_x.at[i, j], sum_x.at[i, j - 1], target) for j, target in ((1, x_next), (2, x_far), (3, x_prev))]
        for i in range(GROUPS)
    ]

    def advance(chains, own_part, s):
        for steps in chains:
            if s < len(steps):
                step, dest, before = steps[s]
                if s > 0:
                    steps[s - 1][0].wait_recv()
                    before[...] += own_part(dest)[...]
                step.start()

    def end_copy(src, dst, arrived, target, itself):
        number = next(numbers)
        remote = pltpu.make_async_remote_copy(
            src_ref=src, dst_ref=dst, send_sem=send.at[number], recv_sem=arrived,
            device_id=target, device_id_type=pl.DeviceIdType.MESH,
        )
        return remote, pltpu.make_async_copy(src, dst, arrived), itself

    place_z, place_x = x * 2 + low, pair * 2 + low
    ends_z = [[
        end_copy(
            own_z.at[i, half], end_z.at[place_z], fin_z.at[place_z],
            device_at(i, odd, 2 * pair + h, core, half), self_z & (x == i) & (core == half),
        ) for half in range(2)] for i in range(GROUPS)]
    ends_x = [[
        end_copy(
            own_x.at[i], end_x.at[place_x], fin_x.at[place_x],
            device_at(i, odd, 2 * x + h, core, half), self_x & (x == i) & (core == half),
        ) for half in range(2)] for i in range(GROUPS)]

    def start_ends(ends):
        for remote, local, itself in ends:
            @pl.when(itself)
            def _():
                local.start()

            @pl.when(jnp.logical_not(itself))
            def _():
                remote.start()

    def wait_ends(ends):
        for remote, local, itself in ends:
            @pl.when(jnp.logical_not(itself))
            def _():
                remote.wait_send()

    def forward(group):
        yg[group].wait_recv()
        cgf[group].start()

    def second(group):
        cols = wide(group)
        fill_rows(ga.at[1], 2, cols)
        cgf[group].wait_recv()
        fill_rows(ga.at[2], 3, cols)
        total = three_pass(m_hi[...], m_lo[...], a_hi[:, cols], a_lo[:, cols], False)
        for place, j in ((0, 0), (1, 1), (2, 3), (3, 2)):
            for side in range(2):
                lanes = slice(side * LANES, (side + 1) * LANES)
                part_z[group, j * 2 + side] = total[place * 128:place * 128 + 64, lanes]
                part_x[group, j, side] = total[place * 128 + 64:place * 128 + 128, lanes]
        for c in to_x[group]:
            c.start()
        advance(chains_z[group], unit_z(group), 0)

    def along_x(group):
        for c in to_x[group]:
            c.wait_recv()
        total = (part_x[group, 0] + sum_x[group, 0]) + (sum_x[group, 1] + sum_x[group, 2])
        for side in range(2):
            for q in range(4):
                hop_x[group, q * 2 + side] = total[side, q * 16:(q + 1) * 16]
        advance(chains_x[group], unit_x(group), 0)

    def finish_z(group):
        for steps in chains_z[group]:
            steps[-1][0].wait_recv()
        total = unit_z(group)(z)[...] + got_z[group, 3] + got_z[group, 6]
        flipped = total.T
        for half in range(2):
            top = flipped[half * 64:half * 64 + 32]
            bottom = flipped[half * 64 + 32:half * 64 + 64]
            own_z[group, half] = jnp.concatenate([top, bottom], axis=1)
        start_ends(ends_z[group])

    def finish_x(group):
        for steps in chains_x[group]:
            steps[-1][0].wait_recv()
        own_x[group] = hop_x[group, z] + got_x[group, 3] + got_x[group, 6]
        start_ends(ends_x[group])

    def clear_first():
        for c in (*xp, *xm, *xf, cb, cg, *yb, *cbf):
            c.wait_send()

    def clear(group):
        for c in (yg[group], cgf[group], *to_x[group]):
            c.wait_send()
        for steps in (*chains_z[group], *chains_x[group]):
            for step, _, _ in steps:
                step.wait_send()

    when = (20.5, 22.0, 24.5, 27.2)
    events = []
    for i in range(GROUPS):
        if i > 0:
            events.append((when[i] - 1.5, forward, (i,)))
        events.append((when[i], second, (i,)))
        for s in range(1, 4):
            events.append((when[i] + 2.2 * s, advance, (chains_z[i], unit_z(i), s)))
        events.append((when[i] + 8.8, finish_z, (i,)))
        events.append((when[i] + 3.9, along_x, (i,)))
        for s in range(1, 4):
            events.append((when[i] + 3.9 + 1.5 * s, advance, (chains_x[i], unit_x(i), s)))
        events.append((when[i] + 9.9, finish_x, (i,)))
        events.append((when[i] + 11.5, clear, (i,)))
    events.append((when[3] + 4.5, clear_first, ()))
    for _, action, arguments in sorted(events, key=lambda e: e[0]):
        action(*arguments)

    def arrived(refs, sems):
        for place in range(8):
            pltpu.make_async_copy(refs.at[place], refs.at[place], sems.at[place]).wait()

    arrived(end_z, fin_z)
    total = end_z[0]
    for place in range(1, 8):
        total = total + end_z[place]
    first = jnp.concatenate([total[:, :64], total[:, 64:]], axis=0)
    arrived(end_x, fin_x)
    pieces = [end_x[q * 2] + end_x[q * 2 + 1] for q in range(4)]
    turn[...] = jnp.concatenate(pieces, axis=0).T
    second_half = turn[pl.ds(pl.multiple_of(core * ROWS, ROWS), ROWS), :]
    for p in range(2):
        lanes = slice(p * 32, p * 32 + 32)
        out_ref[p] = jnp.concatenate([first[:, lanes], second_half[:, lanes]], axis=1)

    for i in range(GROUPS):
        wait_ends(ends_z[i])
        wait_ends(ends_x[i])


def body(green, green_bar):
    f32, bf16 = jnp.float32, jnp.bfloat16
    far = pl.BlockSpec(memory_space=pltpu.HBM)
    return pl.pallas_call(
        kernel,
        out_shape=jax.ShapeDtypeStruct((2, ROWS, ROWS), f32),
        in_specs=[far, far],
        out_specs=pl.BlockSpec(memory_space=pltpu.VMEM),
        scratch_shapes=[
            pltpu.VMEM((2, ROWS, N), f32),
            pltpu.VMEM((2, ROWS, N), f32),
            pltpu.VMEM((3, 2, ROWS, N), f32),
            pltpu.VMEM((3, 2, ROWS, N), f32),
            pltpu.VMEM((3, 2, ROWS, N), f32),
            pltpu.VMEM((512, 2 * N), bf16),
            pltpu.VMEM((512, 2 * N), bf16),
            pltpu.VMEM((256, 2 * N), bf16),
            pltpu.VMEM((256, 2 * N), bf16),
            pltpu.VMEM((512, 512), bf16),
            pltpu.VMEM((512, 512), bf16),
            pltpu.VMEM((512, N), bf16),
            pltpu.VMEM((512, N), bf16),
            pltpu.VMEM((GROUPS, Z, 64, LANES), f32),
            pltpu.VMEM((GROUPS, X, 2, 64, LANES), f32),
            pltpu.VMEM((GROUPS, HOPS, 64, LANES), f32),
            pltpu.VMEM((GROUPS, HOPS, 16, LANES), f32),
            pltpu.VMEM((GROUPS, 3, 2, 64, LANES), f32),
            pltpu.VMEM((GROUPS, Z, 16, LANES), f32),
            pltpu.VMEM((GROUPS, 2, 32, LANES), f32),
            pltpu.VMEM((GROUPS, 16, LANES), f32),
            pltpu.VMEM((8, 32, LANES), f32),
            pltpu.VMEM((8, 16, LANES), f32),
            pltpu.VMEM((LANES, 64), f32),
            pltpu.SemaphoreType.DMA((COPIES,)),
            pltpu.SemaphoreType.DMA((COPIES,)),
            pltpu.SemaphoreType.DMA((8,)),
            pltpu.SemaphoreType.DMA((8,)),
            pltpu.SemaphoreType.DMA((2,)),
        ],
        compiler_params=pltpu.CompilerParams(
            collective_id=0, has_side_effects=True, vmem_limit_bytes=48 * 1024 * 1024
        ),
        cost_estimate=pl.CostEstimate(flops=3 * 1073741824, bytes_accessed=1081344, transcendentals=0),
        name="dyson_adjoint",
    )(green, green_bar)


def solution(mesh):
    spec = P("freq", None, "orb", None)
    return jax.shard_map(
        body, mesh=mesh, in_specs=(spec, spec), out_specs=P(None, "orb", "freq"), check_vma=False
    )
```

time: 73.1 us -> 72.8 us (level)
  no operation moved by 1% of the time
where the time goes in v2:
time: 72.8 us; the launch traced here: 72.5 us
  Pallas kernels  69.8 us (96%)
  local copies, waits for them, and re-layouts  2.71 us (4%)
    pallas_call x1, Pallas kernels, body(): pl.pallas_call(kernel, out_shape=jax.ShapeDtypeStruct((2, ROWS, ROWS), f3...  69.8 us
    unnamed x5, local copies, waits for them, and re-layouts  2.71 us

profile of v2, /device:TPU:39, one launch (start us, length us, event | category | flops | bytes accessed | tf_op | source)
XLA Modules:
  0.0 72.5 jit_solution(1523799876133238914)
XLA Ops:
  0.0 0.0 copy-start
  0.0 1.0 %copy-done = f32[1,2,64,1024]{3,2,1,0:T(8,128)S(1)} copy-done((f32[1,2,64,1024]{3,2,1,0:T(8,128)S(1)}, f32[1,2,64,1024]{3,2,1,0:T(8,128)}, u32[]{:S(2)}) %copy-start) | copy-done | bytes 524312
  1.0 0.0 copy-start.1
  1.0 1.0 %copy-done.1 = f32[1,2,64,1024]{3,2,1,0:T(8,128)S(1)} copy-done((f32[1,2,64,1024]{3,2,1,0:T(8,128)S(1)}, f32[1,2,64,1024]{3,2,1,0:T(8,128)}, u32[]{:S(2)}) %copy-start.1) | copy-done | bytes 524312
  2.1 69.8 %dyson_adjoint.1 = f32[2,64,64]{2,1,0:T(8,128)S(1)} custom-call(f32[1,2,64,1024]{3,2,1,0:T(8,128)S(1)} %copy-done, f32[1,2,64,1024]{3,2,1,0:T(8,128)S(1)} %copy-done.1), custom_call_target="tpu_custom_call" | custom-call | flops 3221225472 | bytes 1081344 | tf_op jit(solution)/shard_map/dyson_adjoint/pallas_call | solution.py:354
  71.9 0.6 copy.4
Async XLA Ops:
  0.0 1.0 %copy-start = (f32[1,2,64,1024]{3,2,1,0:T(8,128)S(1)}, f32[1,2,64,1024]{3,2,1,0:T(8,128)}, u32[]{:S(2)}) copy-start(f32[1,2,64,1024]{3,2,1,0:T(8,128)} %g_hbm.1) | copy-start | bytes 1572868
  1.0 1.0 %copy-start.1 = (f32[1,2,64,1024]{3,2,1,0:T(8,128)S(1)}, f32[1,2,64,1024]{3,2,1,0:T(8,128)}, u32[]{:S(2)}) copy-start(f32[1,2,64,1024]{3,2,1,0:T(8,128)} %b_hbm.1) | copy-start | bytes 1572868

commit v3 on v2

--- a/solution.py
+++ b/solution.py
@@ -7,12 +7,13 @@
 
 ROWS = 64
 N = 1024
-GROUPS = 4
+QUARTERS = 4
+GROUPS = ((0, 2), (2, 1), (3, 1))
 WIDE = 256
 LANES = 128
 X, Z = 4, 8
 HOPS = 7
-COPIES = 120
+COPIES = 112
 
 
 def split(value):
@@ -41,7 +42,7 @@
     g_hbm, b_hbm, out_ref,
     g, b, gc, ba, ga, l_hi, l_lo, w_hi, w_lo, m_hi, m_lo, a_hi, a_lo,
     part_z, part_x, got_z, got_x, sum_x, hop_x, own_z, own_x, end_z, end_x, turn,
-    send, recv, fin_z, fin_x, load,
+    send, recv, fin_z, fin_x, load, nods,
 ):
     freq, orb = lax.axis_index("freq"), lax.axis_index("orb")
     z, low = freq // 2, freq % 2
@@ -75,28 +76,18 @@
     def greet(target):
         pl.semaphore_signal(barrier, inc=1, device_id=target, device_id_type=pl.DeviceIdType.MESH)
 
-    def greet_unless(itself, target):
-        @pl.when(jnp.logical_not(itself))
-        def _():
-            greet(target)
-
-    for target in (x_next, x_prev, x_far, partner, other, z_next, z_prev):
+    twin = device_at(x, h, z, 1 - low, core)
+    for target in (x_next, x_prev, partner, other, z_next, z_prev, twin):
         greet(target)
     self_z = (h == odd) & (low == core)
     self_x = self_z & (x == pair)
-    for from_x in range(X):
-        for from_low in range(2):
-            greet_unless(
-                self_z & (x == from_x) & (low == from_low),
-                device_at(from_x, odd, 2 * pair + h, from_low, low),
+    pl.semaphore_wait(barrier, 7)
+
+    def nod(number, *targets):
+        for target in targets:
+            pl.semaphore_signal(
+                nods.at[number], inc=1, device_id=target, device_id_type=pl.DeviceIdType.MESH
             )
-    for from_pair in range(Z // 2):
-        for from_low in range(2):
-            greet_unless(
-                self_x & (pair == from_pair) & (low == from_low),
-                device_at(pair, odd, 2 * from_pair + h, from_low, low),
-            )
-    pl.semaphore_wait(barrier, 23 - self_z.astype(jnp.int32) - self_x.astype(jnp.int32))
 
     def wide(group):
         return pl.ds(group * WIDE, WIDE)
@@ -107,12 +98,12 @@
     xm = [copy(gh.at[p], gc.at[1, p], x_prev) for p in range(2)]
     cb = copy(bh, ba.at[0], other)
     cg = copy(gh, ga.at[0], other)
-    yg = [copy(gh.at[:, :, wide(i)], ga.at[1, :, :, wide(i)], partner) for i in range(GROUPS)]
+    yg = [copy(gh.at[:, :, wide(i)], ga.at[1, :, :, wide(i)], partner) for i in range(QUARTERS)]
     for c in (yb[0], xp[0], xm[1], cb, yb[1], xp[1], xm[0], cg, *yg):
         c.start()
     xf = [copy(gc.at[0, 0], gc.at[2, 0], x_next), copy(gc.at[1, 1], gc.at[2, 1], x_prev)]
     cbf = [copy(ba.at[1, p], ba.at[2, p], other) for p in range(2)]
-    cgf = [copy(ga.at[1, :, :, wide(i)], ga.at[2, :, :, wide(i)], other) for i in range(GROUPS)]
+    cgf = [copy(ga.at[1, :, :, wide(i)], ga.at[2, :, :, wide(i)], other) for i in range(QUARTERS)]
 
     def fill_left(ref, place):
         high_r, low_r = split(ref[0])
@@ -147,6 +138,7 @@
                 m_hi[rows, :256], m_lo[rows, :256] = split(first)
                 m_hi[rows, 256:], m_lo[rows, 256:] = split(second)
 
+    nod(0, z_next, z_prev)
     load_g.wait()
     fill_left(g, 0)
     fill_rows(g, 0, pl.ds(0, N))
@@ -157,16 +149,21 @@
     cg.wait_recv()
     fill_rows(ga.at[0], 1, pl.ds(0, N))
 
+    pl.semaphore_wait(nods.at[0], 2)
+    nod(1, z_next, z_prev)
     xp[0].wait_recv()
     xf[0].start()
     xm[1].wait_recv()
     xf[1].start()
     yb[0].wait_recv()
     cbf[0].start()
+    pl.semaphore_wait(nods.at[1], 2)
+    nod(2, z_next, z_prev)
     xp[1].wait_recv()
     fill_left(gc.at[0], 2)
     xm[0].wait_recv()
     fill_left(gc.at[1], 1)
+    pl.semaphore_wait(nods.at[2], 2)
     yb[1].wait_recv()
     cbf[1].start()
     fill_bar(ba.at[1], 2)
@@ -181,30 +178,43 @@
     fill_left(gc.at[2], 3)
     middle(3, 1)
 
+    def quarters(group):
+        return pl.ds(*GROUPS[group])
+
     def chains_of(group, own_part, got):
         sign = 1 if group % 2 == 0 else -1
+        at = quarters(group)
         chains = []
         for direction, hops, base in ((sign, 4, 0), (-sign, 3, 4)):
             target = z_next if direction == 1 else z_prev
             steps = []
             for s in range(hops):
                 dest = (z + direction * (hops - s) + Z) % Z
-                before = got.at[group, base + s - 1]
-                steps.append((copy(own_part(dest) if s == 0 else before, got.at[group, base + s], target), dest, before))
+                before = got.at[base + s - 1, at]
+                steps.append((copy(own_part(dest) if s == 0 else before, got.at[base + s, at], target), dest, before))
             chains.append(steps)
         return chains
 
     def unit_z(group):
-        return lambda dest: part_z.at[group, ((dest // 2 - x + X) % X) * 2 + dest % 2]
+        return lambda dest: part_z.at[((dest // 2 - x + X) % X) * 2 + dest % 2, quarters(group)]
 
     def unit_x(group):
-        return lambda dest: hop_x.at[group, dest]
-
-    chains_z = [chains_of(i, unit_z(i), got_z) for i in range(GROUPS)]
-    chains_x = [chains_of(i, unit_x(i), got_x) for i in range(GROUPS)]
+        return lambda dest: hop_x.at[dest, quarters(group)]
+
+    chains_z = [chains_of(i, unit_z(i), got_z) for i in range(len(GROUPS))]
+    direct_x = [
+        [
+            copy(unit_x(i)((z + o) % Z), got_x.at[o - 1, quarters(i)], device_at(x, h, (z + o) % Z, low, core))
+            for o in (4, 3, 5, 2, 6, 1, 7)
+        ]
+        for i in range(len(GROUPS))
+    ]
     to_x = [
-        [copy(part_x.at[i, j], sum_x.at[i, j - 1], target) for j, target in ((1, x_next), (2, x_far), (3, x_prev))]
-        for i in range(GROUPS)
+        [
+            copy(part_x.at[j, quarters(i)], sum_x.at[j - 1, quarters(i)], target)
+            for j, target in ((2, x_far), (1, x_next), (3, x_prev))
+        ]
+        for i in range(len(GROUPS))
     ]
 
     def advance(chains, own_part, s):
@@ -229,12 +239,12 @@
         end_copy(
             own_z.at[i, half], end_z.at[place_z], fin_z.at[place_z],
             device_at(i, odd, 2 * pair + h, core, half), self_z & (x == i) & (core == half),
-        ) for half in range(2)] for i in range(GROUPS)]
+        ) for half in range(2)] for i in range(QUARTERS)]
     ends_x = [[
         end_copy(
             own_x.at[i], end_x.at[place_x], fin_x.at[place_x],
             device_at(i, odd, 2 * x + h, core, half), self_x & (x == i) & (core == half),
-        ) for half in range(2)] for i in range(GROUPS)]
+        ) for half in range(2)] for i in range(QUARTERS)]
 
     def start_ends(ends):
         for remote, local, itself in ends:
@@ -252,21 +262,23 @@
             def _():
                 remote.wait_send()
 
-    def forward(group):
-        yg[group].wait_recv()
-        cgf[group].start()
+    def forward(quarter):
+        yg[quarter].wait_recv()
+        cgf[quarter].start()
 
     def second(group):
-        cols = wide(group)
-        fill_rows(ga.at[1], 2, cols)
-        cgf[group].wait_recv()
-        fill_rows(ga.at[2], 3, cols)
-        total = three_pass(m_hi[...], m_lo[...], a_hi[:, cols], a_lo[:, cols], False)
-        for place, j in ((0, 0), (1, 1), (2, 3), (3, 2)):
-            for side in range(2):
-                lanes = slice(side * LANES, (side + 1) * LANES)
-                part_z[group, j * 2 + side] = total[place * 128:place * 128 + 64, lanes]
-                part_x[group, j, side] = total[place * 128 + 64:place * 128 + 128, lanes]
+        start, count = GROUPS[group]
+        for quarter in range(start, start + count):
+            cols = wide(quarter)
+            fill_rows(ga.at[1], 2, cols)
+            cgf[quarter].wait_recv()
+            fill_rows(ga.at[2], 3, cols)
+            total = three_pass(m_hi[...], m_lo[...], a_hi[:, cols], a_lo[:, cols], False)
+            for place, j in ((0, 0), (1, 1), (2, 3), (3, 2)):
+                for side in range(2):
+                    lanes = slice(side * LANES, (side + 1) * LANES)
+                    part_z[j * 2 + side, quarter] = total[place * 128:place * 128 + 64, lanes]
+                    part_x[j, quarter, side] = total[place * 128 + 64:place * 128 + 128, lanes]
         for c in to_x[group]:
             c.start()
         advance(chains_z[group], unit_z(group), 0)
@@ -274,57 +286,91 @@
     def along_x(group):
         for c in to_x[group]:
             c.wait_recv()
-        total = (part_x[group, 0] + sum_x[group, 0]) + (sum_x[group, 1] + sum_x[group, 2])
-        for side in range(2):
-            for q in range(4):
-                hop_x[group, q * 2 + side] = total[side, q * 16:(q + 1) * 16]
-        advance(chains_x[group], unit_x(group), 0)
+        start, count = GROUPS[group]
+        for i in range(start, start + count):
+            total = (part_x[0, i] + sum_x[0, i]) + (sum_x[1, i] + sum_x[2, i])
+            for side in range(2):
+                for q in range(4):
+                    hop_x[q * 2 + side, i] = total[side, q * 16:(q + 1) * 16]
+        for c in direct_x[group]:
+            c.start()
 
     def finish_z(group):
         for steps in chains_z[group]:
             steps[-1][0].wait_recv()
-        total = unit_z(group)(z)[...] + got_z[group, 3] + got_z[group, 6]
-        flipped = total.T
-        for half in range(2):
-            top = flipped[half * 64:half * 64 + 32]
-            bottom = flipped[half * 64 + 32:half * 64 + 64]
-            own_z[group, half] = jnp.concatenate([top, bottom], axis=1)
-        start_ends(ends_z[group])
+        start, count = GROUPS[group]
+        sums = unit_z(group)(z)[...] + got_z[3, quarters(group)] + got_z[6, quarters(group)]
+        for i in range(count):
+            flipped = sums[i].T
+            for half in range(2):
+                top = flipped[half * 64:half * 64 + 32]
+                bottom = flipped[half * 64 + 32:half * 64 + 64]
+                own_z[start + i, half] = jnp.concatenate([top, bottom], axis=1)
 
     def finish_x(group):
-        for steps in chains_x[group]:
-            steps[-1][0].wait_recv()
-        own_x[group] = hop_x[group, z] + got_x[group, 3] + got_x[group, 6]
-        start_ends(ends_x[group])
+        start, count = GROUPS[group]
+        at = quarters(group)
+        for c in direct_x[group]:
+            c.wait_recv()
+        sums = hop_x[z, at] + got_x[0, at]
+        for o in range(1, 7):
+            sums = sums + got_x[o, at]
+        own_x[at] = sums
+
+    def greet_twin():
+        nod(3, twin)
+
+    def hear_twin():
+        pl.semaphore_wait(nods.at[3], 1)
+
+    def hand_over(ends, group):
+        start, count = GROUPS[group]
+        for i in range(start, start + count):
+            start_ends(ends[i])
 
     def clear_first():
         for c in (*xp, *xm, *xf, cb, cg, *yb, *cbf):
             c.wait_send()
 
     def clear(group):
-        for c in (yg[group], cgf[group], *to_x[group]):
+        for c in to_x[group]:
             c.wait_send()
-        for steps in (*chains_z[group], *chains_x[group]):
+        start, count = GROUPS[group]
+        for i in range(start, start + count):
+            yg[i].wait_send()
+            cgf[i].wait_send()
+        for steps in chains_z[group]:
             for step, _, _ in steps:
                 step.wait_send()
-
-    when = (20.5, 22.0, 24.5, 27.2)
-    events = []
-    for i in range(GROUPS):
-        if i > 0:
-            events.append((when[i] - 1.5, forward, (i,)))
-        events.append((when[i], second, (i,)))
-        for s in range(1, 4):
-            events.append((when[i] + 2.2 * s, advance, (chains_z[i], unit_z(i), s)))
-        events.append((when[i] + 8.8, finish_z, (i,)))
-        events.append((when[i] + 3.9, along_x, (i,)))
-        for s in range(1, 4):
-            events.append((when[i] + 3.9 + 1.5 * s, advance, (chains_x[i], unit_x(i), s)))
-        events.append((when[i] + 9.9, finish_x, (i,)))
-        events.append((when[i] + 11.5, clear, (i,)))
-    events.append((when[3] + 4.5, clear_first, ()))
-    for _, action, arguments in sorted(events, key=lambda e: e[0]):
-        action(*arguments)
+        for c in direct_x[group]:
+            c.wait_send()
+
+    for token in (
+        "F1", "S0", "F2", "S1", "F3", "Z01", "S2", "Z11", "Z02", "Z21", "X0", "Z12", "Z03", "Z22", "X1",
+        "C9", "X2", "Z13", "Z04", "D0", "T0", "Z23", "Z14", "T1", "P0", "Q0", "P1", "Z24", "P2", "C0", "D1",
+        "Q1", "C1", "D2", "Q2", "C2",
+    ):
+        kind, at = token[0], int(token[1])
+        if kind == "F":
+            forward(at)
+        elif kind == "S":
+            second(at)
+        elif kind == "X":
+            along_x(at)
+        elif kind == "D":
+            finish_x(at)
+        elif kind == "T":
+            greet_twin() if at == 0 else hear_twin()
+        elif kind == "P":
+            hand_over(ends_z, at)
+        elif kind == "Q":
+            hand_over(ends_x, at)
+        elif kind == "C":
+            clear(at) if at < len(GROUPS) else clear_first()
+        elif token[2] == "4":
+            finish_z(at)
+        else:
+            advance(chains_z[at], unit_z(at), int(token[2]))
 
     def arrived(refs, sems):
         for place in range(8):
@@ -343,7 +389,7 @@
         lanes = slice(p * 32, p * 32 + 32)
         out_ref[p] = jnp.concatenate([first[:, lanes], second_half[:, lanes]], axis=1)
 
-    for i in range(GROUPS):
+    for i in range(QUARTERS):
         wait_ends(ends_z[i])
         wait_ends(ends_x[i])
 
@@ -370,14 +416,14 @@
             pltpu.VMEM((512, 512), bf16),
             pltpu.VMEM((512, N), bf16),
             pltpu.VMEM((512, N), bf16),
-            pltpu.VMEM((GROUPS, Z, 64, LANES), f32),
-            pltpu.VMEM((GROUPS, X, 2, 64, LANES), f32),
-            pltpu.VMEM((GROUPS, HOPS, 64, LANES), f32),
-            pltpu.VMEM((GROUPS, HOPS, 16, LANES), f32),
-            pltpu.VMEM((GROUPS, 3, 2, 64, LANES), f32),
-            pltpu.VMEM((GROUPS, Z, 16, LANES), f32),
-            pltpu.VMEM((GROUPS, 2, 32, LANES), f32),
-            pltpu.VMEM((GROUPS, 16, LANES), f32),
+            pltpu.VMEM((Z, QUARTERS, 64, LANES), f32),
+            pltpu.VMEM((X, QUARTERS, 2, 64, LANES), f32),
+            pltpu.VMEM((HOPS, QUARTERS, 64, LANES), f32),
+            pltpu.VMEM((HOPS, QUARTERS, 16, LANES), f32),
+            pltpu.VMEM((3, QUARTERS, 2, 64, LANES), f32),
+            pltpu.VMEM((Z, QUARTERS, 16, LANES), f32),
+            pltpu.VMEM((QUARTERS, 2, 32, LANES), f32),
+            pltpu.VMEM((QUARTERS, 16, LANES), f32),
             pltpu.VMEM((8, 32, LANES), f32),
             pltpu.VMEM((8, 16, LANES), f32),
             pltpu.VMEM((LANES, 64), f32),
@@ -386,9 +432,10 @@
             pltpu.SemaphoreType.DMA((8,)),
             pltpu.SemaphoreType.DMA((8,)),
             pltpu.SemaphoreType.DMA((2,)),
+            pltpu.SemaphoreType.REGULAR((4,)),
         ],
         compiler_params=pltpu.CompilerParams(
-            collective_id=0, has_side_effects=True, vmem_limit_bytes=48 * 1024 * 1024
+            collective_id=0, has_side_effects=True, vmem_limit_bytes=63 * 1024 * 1024
         ),
         cost_estimate=pl.CostEstimate(flops=3 * 1073741824, bytes_accessed=1081344, transcendentals=0),
         name="dyson_adjoint",

time: 72.8 us -> 63.9 us (0.88)
  Pallas kernels: 69.8 us -> 62.1 us
  local copies, waits for them, and re-layouts: 2.71 us -> 1.47 us
    pallas_call x1, Pallas kernels: 69.8 us -> 62.1 us  [body(): pl.pallas_call(kernel, out_shape=jax.ShapeDtypeStruct((2, ROWS, ROWS), f3...]
    unnamed x5 -> x1, local copies, waits for them, and re-layouts: 2.71 us -> 1.47 us
where the time goes in v3:
time: 63.9 us; the launch traced here: 63.6 us
  Pallas kernels  62.1 us (97%)
  local copies, waits for them, and re-layouts  1.47 us (2%)
    pallas_call x1, Pallas kernels, body(): pl.pallas_call(kernel, out_shape=jax.ShapeDtypeStruct((2, ROWS, ROWS), f3...  62.1 us
    unnamed x1, local copies, waits for them, and re-layouts  1.47 us

profile of v3, /device:TPU:39, one launch (start us, length us, event | category | flops | bytes accessed | tf_op | source)
XLA Modules:
  0.0 63.6 jit_solution(9525257342630493053)
XLA Ops:
  0.0 62.1 %dyson_adjoint.1 = f32[2,64,64]{2,1,0:T(8,128)} custom-call(f32[1,2,64,1024]{3,2,1,0:T(8,128)} %g_hbm.1, f32[1,2,64,1024]{3,2,1,0:T(8,128)} %b_hbm.1), custom_call_target="tpu_custom_call" | custom-call | flops 3221225472 | bytes 1081344 | tf_op jit(solution)/shard_map/dyson_adjoint/pallas_call | solution.py:400
  62.1 1.5 %copy.4 = f32[2,64,64]{2,1,0:T(8,128)} copy(f32[2,64,64]{2,1,0:T(8,128)} %dyson_adjoint.1) | data formatting | bytes 65536

commit v4 on v3

--- a/solution.py
+++ b/solution.py
@@ -8,12 +8,12 @@
 ROWS = 64
 N = 1024
 QUARTERS = 4
-GROUPS = ((0, 2), (2, 1), (3, 1))
+GROUPS = ((0, 1), (1, 1), (2, 1), (3, 1))
 WIDE = 256
 LANES = 128
 X, Z = 4, 8
 HOPS = 7
-COPIES = 112
+COPIES = 160
 
 
 def split(value):
@@ -41,7 +41,7 @@
 def kernel(
     g_hbm, b_hbm, out_ref,
     g, b, gc, ba, ga, l_hi, l_lo, w_hi, w_lo, m_hi, m_lo, a_hi, a_lo,
-    part_z, part_x, got_z, got_x, sum_x, hop_x, own_z, own_x, end_z, end_x, turn,
+    part_z, part_x, got_z, got_x, sum_x, mid_x, sum_y, hop_x, own_z, own_x, end_z, end_x, turn,
     send, recv, fin_z, fin_x, load, nods,
 ):
     freq, orb = lax.axis_index("freq"), lax.axis_index("orb")
@@ -80,7 +80,6 @@
     for target in (x_next, x_prev, partner, other, z_next, z_prev, twin):
         greet(target)
     self_z = (h == odd) & (low == core)
-    self_x = self_z & (x == pair)
     pl.semaphore_wait(barrier, 7)
 
     def nod(number, *targets):
@@ -89,8 +88,13 @@
                 nods.at[number], inc=1, device_id=target, device_id_type=pl.DeviceIdType.MESH
             )
 
-    def wide(group):
-        return pl.ds(group * WIDE, WIDE)
+    def wide(quarter):
+        return pl.ds(quarter * WIDE, WIDE)
+
+    def lanes_of(quarter, side):
+        return pl.ds((quarter + 2 * side) % QUARTERS * WIDE + side * LANES, LANES)
+
+    blocks = [[lanes_of(i, side) for side in range(2)] for i in range(QUARTERS)]
 
     gh, bh = g_hbm.at[0], b_hbm.at[0]
     yb = [copy(bh.at[p], ba.at[1, p], partner) for p in range(2)]
@@ -98,12 +102,12 @@
     xm = [copy(gh.at[p], gc.at[1, p], x_prev) for p in range(2)]
     cb = copy(bh, ba.at[0], other)
     cg = copy(gh, ga.at[0], other)
-    yg = [copy(gh.at[:, :, wide(i)], ga.at[1, :, :, wide(i)], partner) for i in range(QUARTERS)]
-    for c in (yb[0], xp[0], xm[1], cb, yb[1], xp[1], xm[0], cg, *yg):
+    yg = [[copy(gh.at[:, :, k], ga.at[1, :, :, k], partner) for k in block] for block in blocks]
+    for c in (yb[0], xp[0], xm[1], cb, yb[1], xp[1], xm[0], cg, *sum(yg, [])):
         c.start()
     xf = [copy(gc.at[0, 0], gc.at[2, 0], x_next), copy(gc.at[1, 1], gc.at[2, 1], x_prev)]
     cbf = [copy(ba.at[1, p], ba.at[2, p], other) for p in range(2)]
-    cgf = [copy(ga.at[1, :, :, wide(i)], ga.at[2, :, :, wide(i)], other) for i in range(QUARTERS)]
+    cgf = [[copy(ga.at[1, :, :, k], ga.at[2, :, :, k], other) for k in block] for block in blocks]
 
     def fill_left(ref, place):
         high_r, low_r = split(ref[0])
@@ -123,10 +127,12 @@
         for p in range(2):
             w_hi[rows, pl.ds(p * N, N)], w_lo[rows, pl.ds(p * N, N)] = split(ref[p])
 
-    def fill_rows(ref, slot, columns):
+    def fill_rows(ref, slot, quarter):
         for p in range(2):
             rows = pl.ds(p * 256 + slot * ROWS, ROWS)
-            a_hi[rows, columns], a_lo[rows, columns] = split(ref[p, :, columns])
+            for side in range(2):
+                columns = pl.ds(quarter * WIDE + side * LANES, LANES)
+                a_hi[rows, columns], a_lo[rows, columns] = split(ref[p, :, blocks[quarter][side]])
 
     def middle(start, count):
         rows = pl.ds(start * 128, count * 128)
@@ -141,38 +147,51 @@
     nod(0, z_next, z_prev)
     load_g.wait()
     fill_left(g, 0)
-    fill_rows(g, 0, pl.ds(0, N))
+    for i in range(QUARTERS):
+        fill_rows(g, 0, i)
     load_b.wait()
     fill_bar(b, 0)
     cb.wait_recv()
     fill_bar(ba.at[0], 1)
     cg.wait_recv()
-    fill_rows(ga.at[0], 1, pl.ds(0, N))
+    for i in range(QUARTERS):
+        fill_rows(ga.at[0], 1, i)
 
     pl.semaphore_wait(nods.at[0], 2)
     nod(1, z_next, z_prev)
+    nod(3, other)
     xp[0].wait_recv()
     xf[0].start()
     xm[1].wait_recv()
     xf[1].start()
+    pl.semaphore_wait(nods.at[3], 1)
+    nod(4, partner)
     yb[0].wait_recv()
     cbf[0].start()
     pl.semaphore_wait(nods.at[1], 2)
     nod(2, z_next, z_prev)
+    pl.semaphore_wait(nods.at[4], 1)
+    nod(5, twin)
+    pl.semaphore_wait(nods.at[5], 1)
+    nod(6, x_next, x_prev)
     xp[1].wait_recv()
     fill_left(gc.at[0], 2)
     xm[0].wait_recv()
     fill_left(gc.at[1], 1)
     pl.semaphore_wait(nods.at[2], 2)
+    pl.semaphore_wait(nods.at[6], 2)
+    nod(7, x_next, x_prev)
     yb[1].wait_recv()
     cbf[1].start()
     fill_bar(ba.at[1], 2)
     for c in cbf:
         c.wait_recv()
     fill_bar(ba.at[2], 3)
+    pl.semaphore_wait(nods.at[7], 2)
     middle(0, 3)
-    yg[0].wait_recv()
-    cgf[0].start()
+    for side in range(2):
+        yg[0][side].wait_recv()
+        cgf[0][side].start()
     for c in xf:
         c.wait_recv()
     fill_left(gc.at[2], 3)
@@ -209,9 +228,10 @@
         ]
         for i in range(len(GROUPS))
     ]
+    to_twin = [copy(mid_x.at[1 - low, quarters(i)], sum_y.at[quarters(i)], twin) for i in range(len(GROUPS))]
     to_x = [
         [
-            copy(part_x.at[j, quarters(i)], sum_x.at[j - 1, quarters(i)], target)
+            copy(part_x.at[(x + j) % X, quarters(i)], sum_x.at[j - 1, quarters(i)], target)
             for j, target in ((2, x_far), (1, x_next), (3, x_prev))
         ]
         for i in range(len(GROUPS))
@@ -234,16 +254,18 @@
         )
         return remote, pltpu.make_async_copy(src, dst, arrived), itself
 
-    place_z, place_x = x * 2 + low, pair * 2 + low
+    place_z = place_x = x * 2 + low
     ends_z = [[
         end_copy(
             own_z.at[i, half], end_z.at[place_z], fin_z.at[place_z],
-            device_at(i, odd, 2 * pair + h, core, half), self_z & (x == i) & (core == half),
+            device_at((i + 2 * odd) % X, odd, 2 * pair + h, core, half),
+            self_z & (x == (i + 2 * odd) % X) & (core == half),
         ) for half in range(2)] for i in range(QUARTERS)]
     ends_x = [[
         end_copy(
             own_x.at[i], end_x.at[place_x], fin_x.at[place_x],
-            device_at(i, odd, 2 * x + h, core, half), self_x & (x == i) & (core == half),
+            device_at((i + 2 * odd) % X, odd, 2 * pair + h, core, half),
+            self_z & (x == (i + 2 * odd) % X) & (core == half),
         ) for half in range(2)] for i in range(QUARTERS)]
 
     def start_ends(ends):
@@ -263,22 +285,26 @@
                 remote.wait_send()
 
     def forward(quarter):
-        yg[quarter].wait_recv()
-        cgf[quarter].start()
+        for side in range(2):
+            yg[quarter][side].wait_recv()
+            cgf[quarter][side].start()
 
     def second(group):
         start, count = GROUPS[group]
         for quarter in range(start, start + count):
             cols = wide(quarter)
-            fill_rows(ga.at[1], 2, cols)
-            cgf[quarter].wait_recv()
-            fill_rows(ga.at[2], 3, cols)
+            fill_rows(ga.at[1], 2, quarter)
+            for c in cgf[quarter]:
+                c.wait_recv()
+            fill_rows(ga.at[2], 3, quarter)
             total = three_pass(m_hi[...], m_lo[...], a_hi[:, cols], a_lo[:, cols], False)
             for place, j in ((0, 0), (1, 1), (2, 3), (3, 2)):
                 for side in range(2):
                     lanes = slice(side * LANES, (side + 1) * LANES)
                     part_z[j * 2 + side, quarter] = total[place * 128:place * 128 + 64, lanes]
-                    part_x[j, quarter, side] = total[place * 128 + 64:place * 128 + 128, lanes]
+                    for k in range(X):
+                        rows = place * 128 + 64 + k * 16
+                        part_x[k, quarter, 2 * ((x + j) % X) + side] = total[rows:rows + 16, lanes]
         for c in to_x[group]:
             c.start()
         advance(chains_z[group], unit_z(group), 0)
@@ -288,10 +314,16 @@
             c.wait_recv()
         start, count = GROUPS[group]
         for i in range(start, start + count):
-            total = (part_x[0, i] + sum_x[0, i]) + (sum_x[1, i] + sum_x[2, i])
-            for side in range(2):
-                for q in range(4):
-                    hop_x[q * 2 + side, i] = total[side, q * 16:(q + 1) * 16]
+            total = (part_x[x, i] + sum_x[0, i]) + (sum_x[1, i] + sum_x[2, i])
+            for part in range(2):
+                mid_x[part, i] = total[:, part * 8:part * 8 + 8]
+        to_twin[group].start()
+
+    def along_y(group):
+        to_twin[group].wait_recv()
+        start, count = GROUPS[group]
+        for i in range(start, start + count):
+            hop_x[:, i] = mid_x[low, i] + sum_y[i]
         for c in direct_x[group]:
             c.start()
 
@@ -317,12 +349,6 @@
             sums = sums + got_x[o, at]
         own_x[at] = sums
 
-    def greet_twin():
-        nod(3, twin)
-
-    def hear_twin():
-        pl.semaphore_wait(nods.at[3], 1)
-
     def hand_over(ends, group):
         start, count = GROUPS[group]
         for i in range(start, start + count):
@@ -337,18 +363,19 @@
             c.wait_send()
         start, count = GROUPS[group]
         for i in range(start, start + count):
-            yg[i].wait_send()
-            cgf[i].wait_send()
+            for c in (*yg[i], *cgf[i]):
+                c.wait_send()
         for steps in chains_z[group]:
             for step, _, _ in steps:
                 step.wait_send()
+        to_twin[group].wait_send()
         for c in direct_x[group]:
             c.wait_send()
 
     for token in (
-        "F1", "S0", "F2", "S1", "F3", "Z01", "S2", "Z11", "Z02", "Z21", "X0", "Z12", "Z03", "Z22", "X1",
-        "C9", "X2", "Z13", "Z04", "D0", "T0", "Z23", "Z14", "T1", "P0", "Q0", "P1", "Z24", "P2", "C0", "D1",
-        "Q1", "C1", "D2", "Q2", "C2",
+        "F1", "S0", "F2", "S1", "F3", "Z01", "S2", "Z11", "X0", "S3", "Z02", "Z21", "X1", "Z12", "Y0", "Z31",
+        "X2", "Z03", "C9", "Z22", "Y1", "X3", "Z13", "Z32", "Y2", "D0", "Q0", "Z04", "P0", "Z23", "Y3", "D1",
+        "Q1", "Z14", "P1", "Z33", "D2", "Q2", "D3", "Q3", "Z24", "P2", "Z34", "P3", "C0", "C1", "C2", "C3",
     ):
         kind, at = token[0], int(token[1])
         if kind == "F":
@@ -357,10 +384,10 @@
             second(at)
         elif kind == "X":
             along_x(at)
+        elif kind == "Y":
+            along_y(at)
         elif kind == "D":
             finish_x(at)
-        elif kind == "T":
-            greet_twin() if at == 0 else hear_twin()
         elif kind == "P":
             hand_over(ends_z, at)
         elif kind == "Q":
@@ -382,8 +409,7 @@
         total = total + end_z[place]
     first = jnp.concatenate([total[:, :64], total[:, 64:]], axis=0)
     arrived(end_x, fin_x)
-    pieces = [end_x[q * 2] + end_x[q * 2 + 1] for q in range(4)]
-    turn[...] = jnp.concatenate(pieces, axis=0).T
+    turn[...] = end_x[...].reshape(64, LANES).T
     second_half = turn[pl.ds(pl.multiple_of(core * ROWS, ROWS), ROWS), :]
     for p in range(2):
         lanes = slice(p * 32, p * 32 + 32)
@@ -417,22 +443,24 @@
             pltpu.VMEM((512, N), bf16),
             pltpu.VMEM((512, N), bf16),
             pltpu.VMEM((Z, QUARTERS, 64, LANES), f32),
-            pltpu.VMEM((X, QUARTERS, 2, 64, LANES), f32),
+            pltpu.VMEM((X, QUARTERS, Z, 16, LANES), f32),
             pltpu.VMEM((HOPS, QUARTERS, 64, LANES), f32),
-            pltpu.VMEM((HOPS, QUARTERS, 16, LANES), f32),
-            pltpu.VMEM((3, QUARTERS, 2, 64, LANES), f32),
-            pltpu.VMEM((Z, QUARTERS, 16, LANES), f32),
+            pltpu.VMEM((HOPS, QUARTERS, 8, LANES), f32),
+            pltpu.VMEM((3, QUARTERS, Z, 16, LANES), f32),
+            pltpu.VMEM((2, QUARTERS, Z, 8, LANES), f32),
+            pltpu.VMEM((QUARTERS, Z, 8, LANES), f32),
+            pltpu.VMEM((Z, QUARTERS, 8, LANES), f32),
             pltpu.VMEM((QUARTERS, 2, 32, LANES), f32),
-            pltpu.VMEM((QUARTERS, 16, LANES), f32),
+            pltpu.VMEM((QUARTERS, 8, LANES), f32),
             pltpu.VMEM((8, 32, LANES), f32),
-            pltpu.VMEM((8, 16, LANES), f32),
+            pltpu.VMEM((8, 8, LANES), f32),
             pltpu.VMEM((LANES, 64), f32),
             pltpu.SemaphoreType.DMA((COPIES,)),
             pltpu.SemaphoreType.DMA((COPIES,)),
             pltpu.SemaphoreType.DMA((8,)),
             pltpu.SemaphoreType.DMA((8,)),
             pltpu.SemaphoreType.DMA((2,)),
-            pltpu.SemaphoreType.REGULAR((4,)),
+            pltpu.SemaphoreType.REGULAR((8,)),
         ],
         compiler_params=pltpu.CompilerParams(
             collective_id=0, has_side_effects=True, vmem_limit_bytes=63 * 1024 * 1024

time: 63.9 us -> 62.4 us (0.977)
  Pallas kernels: 62.1 us -> 60.7 us
    pallas_call x1, Pallas kernels: 62.1 us -> 60.7 us  [body(): pl.pallas_call(kernel, out_shape=jax.ShapeDtypeStruct((2, ROWS, ROWS), f3...]
where the time goes in v4:
time: 62.4 us; the launch traced here: 62.2 us
  Pallas kernels  60.7 us (97%)
  local copies, waits for them, and re-layouts  1.47 us (2%)
    pallas_call x1, Pallas kernels, body(): pl.pallas_call(kernel, out_shape=jax.ShapeDtypeStruct((2, ROWS, ROWS), f3...  60.7 us
    unnamed x1, local copies, waits for them, and re-layouts  1.47 us

profile of v4, /device:TPU:39, one launch (start us, length us, event | category | flops | bytes accessed | tf_op | source)
XLA Modules:
  0.0 62.2 jit_solution(11754307218032935856)
XLA Ops:
  0.0 60.7 %dyson_adjoint.1 = f32[2,64,64]{2,1,0:T(8,128)} custom-call(f32[1,2,64,1024]{3,2,1,0:T(8,128)} %g_hbm.1, f32[1,2,64,1024]{3,2,1,0:T(8,128)} %b_hbm.1), custom_call_target="tpu_custom_call" | custom-call | flops 3221225472 | bytes 1081344 | tf_op jit(solution)/shard_map/dyson_adjoint/pallas_call | solution.py:426
  60.8 1.5 %copy.4 = f32[2,64,64]{2,1,0:T(8,128)} copy(f32[2,64,64]{2,1,0:T(8,128)} %dyson_adjoint.1) | data formatting | bytes 65536

commit v5 on v4

--- a/solution.py
+++ b/solution.py
@@ -373,9 +373,10 @@
             c.wait_send()
 
     for token in (
-        "F1", "S0", "F2", "S1", "F3", "Z01", "S2", "Z11", "X0", "S3", "Z02", "Z21", "X1", "Z12", "Y0", "Z31",
-        "X2", "Z03", "C9", "Z22", "Y1", "X3", "Z13", "Z32", "Y2", "D0", "Q0", "Z04", "P0", "Z23", "Y3", "D1",
-        "Q1", "Z14", "P1", "Z33", "D2", "Q2", "D3", "Q3", "Z24", "P2", "Z34", "P3", "C0", "C1", "C2", "C3",
+        "F1", "S0", "F2", "S1", "F3", "Z01", "S2", "Z11", "X0", "S3", "Z02", "Z21", "X1", "Z12", "Z31", "Y0",
+        "X2", "Z03", "Z22", "C9", "Y1", "X3", "Z13", "Z32", "Y2", "Z04", "P0", "D0", "Q0", "Z23", "Y3",
+        "Z14", "P1", "D1", "Q1", "Z33", "Z24", "P2", "D2", "Q2", "Z34", "P3", "D3", "Q3", "C0", "C1", "C2",
+        "C3",
     ):
         kind, at = token[0], int(token[1])
         if kind == "F":
@@ -463,7 +464,7 @@
             pltpu.SemaphoreType.REGULAR((8,)),
         ],
         compiler_params=pltpu.CompilerParams(
-            collective_id=0, has_side_effects=True, vmem_limit_bytes=63 * 1024 * 1024
+            collective_id=0, has_side_effects=True, vmem_limit_bytes=54912 * 1024
         ),
         cost_estimate=pl.CostEstimate(flops=3 * 1073741824, bytes_accessed=1081344, transcendentals=0),
         name="dyson_adjoint",

time: 62.4 us -> 59.7 us (0.957)
  Pallas kernels: 60.7 us -> 58.9 us
  local copies, waits for them, and re-layouts: 1.47 us -> 0.63 us
    pallas_call x1, Pallas kernels: 60.7 us -> 58.9 us  [body(): pl.pallas_call(kernel, out_shape=jax.ShapeDtypeStruct((2, ROWS, ROWS), f3...]
    unnamed x1, local copies, waits for them, and re-layouts: 1.47 us -> 0.63 us
where the time goes in v5:
time: 59.7 us; the launch traced here: 59.6 us
  Pallas kernels  58.9 us (99%)
  local copies, waits for them, and re-layouts  0.63 us (1%)
    pallas_call x1, Pallas kernels, body(): pl.pallas_call(kernel, out_shape=jax.ShapeDtypeStruct((2, ROWS, ROWS), f3...  58.9 us

profile of v5, /device:TPU:39, one launch (start us, length us, event | category | flops | bytes accessed | tf_op | source)
XLA Modules:
  0.0 59.6 jit_solution(9247221836051617088)
XLA Ops:
  0.0 58.9 %dyson_adjoint.1 = f32[2,64,64]{2,1,0:T(8,128)S(1)} custom-call(f32[1,2,64,1024]{3,2,1,0:T(8,128)} %g_hbm.1, f32[1,2,64,1024]{3,2,1,0:T(8,128)} %b_hbm.1), custom_call_target="tpu_custom_call" | custom-call | flops 3221225472 | bytes 1081344 | tf_op jit(solution)/shard_map/dyson_adjoint/pallas_call | solution.py:427
  59.0 0.6 %copy.4 = f32[2,64,64]{2,1,0:T(8,128)} copy(f32[2,64,64]{2,1,0:T(8,128)S(1)} %dyson_adjoint.1) | data formatting | bytes 65536

commit v6 on v5

--- a/solution.py
+++ b/solution.py
@@ -374,8 +374,8 @@
 
     for token in (
         "F1", "S0", "F2", "S1", "F3", "Z01", "S2", "Z11", "X0", "S3", "Z02", "Z21", "X1", "Z12", "Z31", "Y0",
-        "X2", "Z03", "Z22", "C9", "Y1", "X3", "Z13", "Z32", "Y2", "Z04", "P0", "D0", "Q0", "Z23", "Y3",
-        "Z14", "P1", "D1", "Q1", "Z33", "Z24", "P2", "D2", "Q2", "Z34", "P3", "D3", "Q3", "C0", "C1", "C2",
+        "X2", "Z03", "Z22", "C9", "Y1", "X3", "Z13", "Z32", "Y2", "Z04", "D0", "Z23", "Y3", "Z14", "P0",
+        "Q0", "Z33", "D1", "P1", "Q1", "Z24", "D2", "Z34", "P2", "Q2", "P3", "D3", "Q3", "C0", "C1", "C2",
         "C3",
     ):
         kind, at = token[0], int(token[1])
@@ -404,6 +404,9 @@
         for place in range(8):
             pltpu.make_async_copy(refs.at[place], refs.at[place], sems.at[place]).wait()
 
+    for i in range(QUARTERS - 1):
+        wait_ends(ends_z[i])
+        wait_ends(ends_x[i])
     arrived(end_z, fin_z)
     total = end_z[0]
     for place in range(1, 8):
@@ -416,7 +419,7 @@
         lanes = slice(p * 32, p * 32 + 32)
         out_ref[p] = jnp.concatenate([first[:, lanes], second_half[:, lanes]], axis=1)
 
-    for i in range(QUARTERS):
+    for i in range(QUARTERS - 1, QUARTERS):
         wait_ends(ends_z[i])
         wait_ends(ends_x[i])
 

time: 59.7 us -> 59.3 us (level)
  no operation moved by 1% of the time
where the time goes in v6:
time: 59.3 us; the launch traced here: 59.2 us
  Pallas kernels  58.5 us (99%)
  local copies, waits for them, and re-layouts  0.63 us (1%)
    pallas_call x1, Pallas kernels, body(): pl.pallas_call(kernel, out_shape=jax.ShapeDtypeStruct((2, ROWS, ROWS), f3...  58.5 us

profile of v6, /device:TPU:39, one launch (start us, length us, event | category | flops | bytes accessed | tf_op | source)
XLA Modules:
  0.0 59.2 jit_solution(15894869382838524338)
XLA Ops:
  0.0 58.5 %dyson_adjoint.1 = f32[2,64,64]{2,1,0:T(8,128)S(1)} custom-call(f32[1,2,64,1024]{3,2,1,0:T(8,128)} %g_hbm.1, f32[1,2,64,1024]{3,2,1,0:T(8,128)} %b_hbm.1), custom_call_target="tpu_custom_call" | custom-call | flops 3221225472 | bytes 1081344 | tf_op jit(solution)/shard_map/dyson_adjoint/pallas_call | solution.py:430
  58.5 0.6 %copy.4 = f32[2,64,64]{2,1,0:T(8,128)} copy(f32[2,64,64]{2,1,0:T(8,128)S(1)} %dyson_adjoint.1) | data formatting | bytes 65536

commit v7 on v6

--- a/solution.py
+++ b/solution.py
@@ -305,9 +305,9 @@
                     for k in range(X):
                         rows = place * 128 + 64 + k * 16
                         part_x[k, quarter, 2 * ((x + j) % X) + side] = total[rows:rows + 16, lanes]
+        advance(chains_z[group], unit_z(group), 0)
         for c in to_x[group]:
             c.start()
-        advance(chains_z[group], unit_z(group), 0)
 
     def along_x(group):
         for c in to_x[group]:
@@ -400,19 +400,20 @@
         else:
             advance(chains_z[at], unit_z(at), int(token[2]))
 
-    def arrived(refs, sems):
-        for place in range(8):
-            pltpu.make_async_copy(refs.at[place], refs.at[place], sems.at[place]).wait()
+    def arrived(refs, sems, place):
+        pltpu.make_async_copy(refs.at[place], refs.at[place], sems.at[place]).wait()
 
     for i in range(QUARTERS - 1):
         wait_ends(ends_z[i])
         wait_ends(ends_x[i])
-    arrived(end_z, fin_z)
+    arrived(end_z, fin_z, 0)
     total = end_z[0]
     for place in range(1, 8):
+        arrived(end_z, fin_z, place)
         total = total + end_z[place]
     first = jnp.concatenate([total[:, :64], total[:, 64:]], axis=0)
-    arrived(end_x, fin_x)
+    for place in range(8):
+        arrived(end_x, fin_x, place)
     turn[...] = end_x[...].reshape(64, LANES).T
     second_half = turn[pl.ds(pl.multiple_of(core * ROWS, ROWS), ROWS), :]
     for p in range(2):

time: 59.3 us -> 59.3 us (level)
  no operation moved by 1% of the time
where the time goes in v7:
time: 59.3 us; the launch traced here: 59.2 us
  Pallas kernels  58.5 us (99%)
  local copies, waits for them, and re-layouts  0.63 us (1%)
    pallas_call x1, Pallas kernels, body(): pl.pallas_call(kernel, out_shape=jax.ShapeDtypeStruct((2, ROWS, ROWS), f3...  58.5 us

profile of v7, /device:TPU:39, one launch (start us, length us, event | category | flops | bytes accessed | tf_op | source)
XLA Modules:
  0.0 59.2 jit_solution(5433977244762916718)
XLA Ops:
  0.0 58.5 %dyson_adjoint.1 = f32[2,64,64]{2,1,0:T(8,128)S(1)} custom-call(f32[1,2,64,1024]{3,2,1,0:T(8,128)} %g_hbm.1, f32[1,2,64,1024]{3,2,1,0:T(8,128)} %b_hbm.1), custom_call_target="tpu_custom_call" | custom-call | flops 3221225472 | bytes 1081344 | tf_op jit(solution)/shard_map/dyson_adjoint/pallas_call | solution.py:431
  58.5 0.6 %copy.4 = f32[2,64,64]{2,1,0:T(8,128)} copy(f32[2,64,64]{2,1,0:T(8,128)S(1)} %dyson_adjoint.1) | data formatting | bytes 65536

commit v8 on v7

--- a/solution.py
+++ b/solution.py
@@ -103,7 +103,7 @@
     cb = copy(bh, ba.at[0], other)
     cg = copy(gh, ga.at[0], other)
     yg = [[copy(gh.at[:, :, k], ga.at[1, :, :, k], partner) for k in block] for block in blocks]
-    for c in (yb[0], xp[0], xm[1], cb, yb[1], xp[1], xm[0], cg, *sum(yg, [])):
+    for c in (xp[0], xm[1], yb[0], cb, xp[1], xm[0], yb[1], cg, *sum(yg, [])):
         c.start()
     xf = [copy(gc.at[0, 0], gc.at[2, 0], x_next), copy(gc.at[1, 1], gc.at[2, 1], x_prev)]
     cbf = [copy(ba.at[1, p], ba.at[2, p], other) for p in range(2)]

time: 59.3 us -> 59.3 us (level)
  no operation moved by 1% of the time
where the time goes in v8:
time: 59.3 us; the launch traced here: 59.2 us
  Pallas kernels  58.5 us (99%)
  local copies, waits for them, and re-layouts  0.63 us (1%)
    pallas_call x1, Pallas kernels, body(): pl.pallas_call(kernel, out_shape=jax.ShapeDtypeStruct((2, ROWS, ROWS), f3...  58.5 us

profile of v8, /device:TPU:39, one launch (start us, length us, event | category | flops | bytes accessed | tf_op | source)
XLA Modules:
  0.0 59.2 jit_solution(11465701882690080765)
XLA Ops:
  0.0 58.5 %dyson_adjoint.1 = f32[2,64,64]{2,1,0:T(8,128)S(1)} custom-call(f32[1,2,64,1024]{3,2,1,0:T(8,128)} %g_hbm.1, f32[1,2,64,1024]{3,2,1,0:T(8,128)} %b_hbm.1), custom_call_target="tpu_custom_call" | custom-call | flops 3221225472 | bytes 1081344 | tf_op jit(solution)/shard_map/dyson_adjoint/pallas_call | solution.py:431
  58.5 0.6 %copy.4 = f32[2,64,64]{2,1,0:T(8,128)} copy(f32[2,64,64]{2,1,0:T(8,128)S(1)} %dyson_adjoint.1) | data formatting | bytes 65536
